TPU v7x, 512 devices: a whole 4x8x8 slice. The times are simulated.
512 devices in a mesh: expert: 64 (over x, z, core), dp: 8 (over y).
Axes of the slice: x: 4, y: 8, z: 8, core: 2. Of those that a mesh axis runs over, the one named last changes fastest.
Arguments:
- tokens: bfloat16 [1024, 7168], P('expert'), may hold values from -6 to 6
- teacher_out: bfloat16 [1024, 8, 7168], P('expert', None, 'dp'), may hold values from -4 to 4
- route_weight: bfloat16 [1024, 8], P('expert'), may hold values from 0.049804688 to 0.5
- routes: int32 [1024, 8], P('expert'), may hold values from 0 to 63, all different within a row; in each aligned block of 16 rows (0 to 15, 16 to 31, ...) at most 4 rows name the same one
- twin_map: int32 [64], replicated, may hold values from 0 to 31, as said below
- student_gate: bfloat16 [64, 384, 7168], P('expert', 'dp'), may hold values from -0.0625 to 0.0625
- student_up: bfloat16 [64, 384, 7168], P('expert', 'dp'), may hold values from -0.0625 to 0.0625
- student_down: bfloat16 [64, 384, 7168], P('expert', None, 'dp'), may hold values from -0.21875 to 0.21875
Outputs:
- grad_gate: bfloat16 [64, 384, 7168], P('expert', 'dp')
- grad_up: bfloat16 [64, 384, 7168], P('expert', 'dp')
- grad_down: bfloat16 [64, 384, 7168], P('expert', None, 'dp')
Inputs may be any that keep to these rules, and one draw needn't show every extreme that they name: `routes`: in the 16 tokens held by one device of the expert axis (one routing block) no teacher expert is named more than 4 times, and each token names 8 different teacher experts. `twin_map`: each student number is named by exactly two teacher experts.
All inputs are finite; a program needn't handle non-finite values.
Results may differ from a plain program's by a relative error of at most 0.024.
Values may be sent and summed in bfloat16 or wider, within the bound.
A program may use at most 128 MiB of HBM per device.

v0:
```python
import jax
import jax.numpy as jnp
from jax import lax
from jax.sharding import PartitionSpec as P

last_dims = (((1,), (1,)), ((), ()))
first_dims = (((0,), (0,)), ((), ()))


def partner(block, axis, apart):
    count = lax.axis_size(axis)
    route = []
    for low in range(count):
        high = low | 1 << apart
        if high != low and high < count:
            route += [(low, high), (high, low)]
    return lax.ppermute(block, axis, route)


def slot_table(routes, twin_map, capacity):
    teacher_count = twin_map.shape[0]
    pair_count = routes.shape[0] * routes.shape[1]
    teach_ids = routes.reshape(pair_count)
    teacher_hot = (
        teach_ids[:, None] == jnp.arange(teacher_count, dtype=jnp.int32)[None, :]
    ).astype(jnp.int32)
    same_student = twin_map[:, None] == twin_map[None, :]
    earlier_teach = (
        jnp.arange(teacher_count, dtype=jnp.int32)[None, :]
        < jnp.arange(teacher_count, dtype=jnp.int32)[:, None]
    )
    twin_of = jnp.sum(same_student & earlier_teach, axis=1)
    student_ids = jnp.sum(teacher_hot * twin_map[None, :], axis=1)
    twin_ids = jnp.sum(teacher_hot * twin_of[None, :], axis=1)
    same_teacher = teach_ids[:, None] == teach_ids[None, :]
    earlier_pair = (
        jnp.arange(pair_count, dtype=jnp.int32)[None, :]
        < jnp.arange(pair_count, dtype=jnp.int32)[:, None]
    )
    rank_ids = jnp.sum(same_teacher & earlier_pair, axis=1)
    slot_ids = student_ids * (2 * capacity) + twin_ids * capacity + rank_ids
    slot_total = teacher_count // 2 * 2 * capacity
    return (slot_ids[:, None] == jnp.arange(slot_total, dtype=jnp.int32)[None, :]).astype(
        jnp.bfloat16
    )


def body(
    tokens, teacher_out, route_weight, routes, twin_map, student_gate, student_up, student_down
):
    teacher_count = twin_map.shape[0]
    student_count = teacher_count // 2
    topk_count = routes.shape[1]
    pair_count = routes.shape[0] * topk_count
    capacity = 2 * pair_count // teacher_count
    feature_part = teacher_out.shape[2]
    placing = slot_table(routes, twin_map, capacity)
    row_features = tokens.shape[1]
    pair_rows = jnp.repeat(tokens, topk_count, axis=0)
    send_rows = lax.dot_general(
        placing, pair_rows, first_dims, preferred_element_type=jnp.float32
    ).astype(jnp.bfloat16)
    send_target = lax.dot_general(
        placing,
        teacher_out.reshape(pair_count, feature_part),
        first_dims,
        preferred_element_type=jnp.float32,
    ).astype(jnp.bfloat16)
    send_weight = jnp.dot(
        route_weight.reshape(pair_count), placing, preferred_element_type=jnp.float32
    ).astype(jnp.bfloat16)
    outgoing = (
        jnp.repeat(send_rows.reshape(student_count, 2 * capacity, row_features), 2, axis=0),
        jnp.repeat(send_target.reshape(student_count, 2 * capacity, feature_part), 2, axis=0),
        jnp.repeat(send_weight.reshape(student_count, 2 * capacity), 2, axis=0),
    )
    arrived = (
        lax.all_to_all(outgoing[0], "expert", split_axis=0, concat_axis=0, tiled=True),
        lax.all_to_all(outgoing[1], "expert", split_axis=0, concat_axis=0, tiled=True),
        lax.all_to_all(outgoing[2], "expert", split_axis=0, concat_axis=0, tiled=True),
    )
    slot_rows = arrived[0].reshape(-1, row_features)
    slot_target = arrived[1].reshape(-1, feature_part)
    slot_weight = arrived[2].reshape(-1)
    w_gate = student_gate[0]
    w_up = student_up[0]
    w_down = student_down[0]
    gate_pre = lax.dot_general(slot_rows, w_gate, last_dims, preferred_element_type=jnp.float32)
    up_pre = lax.dot_general(slot_rows, w_up, last_dims, preferred_element_type=jnp.float32)
    sigmoid_gate = jax.nn.sigmoid(gate_pre)
    silu_gate = gate_pre * sigmoid_gate
    hidden = (silu_gate * up_pre).astype(jnp.bfloat16)
    hidden_half = lax.all_gather(hidden, "dp", axis=1, tiled=True)
    half_out = jnp.dot(hidden_half, w_down, preferred_element_type=jnp.float32)
    student_out = half_out + partner(half_out.astype(jnp.bfloat16), "expert", 0).astype(
        half_out.dtype
    )
    error_part = (
        slot_weight.astype(jnp.float32)[:, None] * (student_out - slot_target.astype(jnp.float32))
    ).astype(jnp.bfloat16)
    grad_down = lax.dot_general(
        hidden_half, error_part, first_dims, preferred_element_type=jnp.float32
    ).astype(jnp.bfloat16)
    back_terms = lax.dot_general(error_part, w_down, last_dims, preferred_element_type=jnp.float32)
    back_hidden = lax.psum_scatter(
        back_terms.astype(jnp.bfloat16), "dp", scatter_dimension=1, tiled=True
    ).astype(jnp.float32)
    silu_slope = sigmoid_gate * (1.0 + gate_pre * (1.0 - sigmoid_gate))
    back_gate = (back_hidden * up_pre * silu_slope).astype(jnp.bfloat16)
    back_up = (back_hidden * silu_gate).astype(jnp.bfloat16)
    grad_gate = lax.dot_general(
        back_gate, slot_rows, first_dims, preferred_element_type=jnp.float32
    ).astype(jnp.bfloat16)
    grad_up = lax.dot_general(
        back_up, slot_rows, first_dims, preferred_element_type=jnp.float32
    ).astype(jnp.bfloat16)
    return (grad_gate[None], grad_up[None], grad_down[None])


def solution(mesh):
    placed = (
        P("expert", None),
        P("expert", None, "dp"),
        P("expert", None),
        P("expert", None),
        P(),
        P("expert", "dp", None),
        P("expert", "dp", None),
        P("expert", None, "dp"),
    )
    return jax.shard_map(
        body,
        mesh=mesh,
        in_specs=placed,
        out_specs=(P("expert", "dp", None), P("expert", "dp", None), P("expert", None, "dp")),
        check_vma=False,
    )
```

profile of v0, /device:TPU:1, one launch (start us, length us, event | category | flops | bytes accessed | tf_op | source)
XLA Modules:
  0.0 312.4 jit_solution(3041398293528733679)
XLA Ops:
  7.2 0.8 copy.20
  8.1 0.9 convert_reduce_fusion.2
  9.2 0.8 select_reduce_fusion.1
  10.0 2.2 fusion
  12.1 3.9 %broadcast_in_dim.16 = bf16[32,2,8,7168]{3,2,1,0:T(8,128)(2,1)} broadcast(bf16[32,8,7168]{2,1,0:T(8,128)(2,1)S(1)} %fusion), dimensions={0,2,3} | broadcast | bytes 11010048 | tf_op jit(solution)/shard_map/broadcast_in_dim | solution.py:73
  16.0 15.1 %all-to-all-start.1 = ((bf16[64,8,7168]{2,1,0:T(8,128)(2,1)}), bf16[64,8,7168]{2,1,0:T(8,128)(2,1)}, u32[]{:S(2)}, u32[]{:S(2)}) async-start(bf16[64,8,7168]{2,1,0:T(8,128)(2,1)} %bitcast.54), calls=%async_computation.1 | async-start | bytes 14680064 | tf_op jit(solution)/shard_map/all_to_all | solution.py:78
  32.8 161.7 %all-to-all-done.1 = bf16[64,8,7168]{2,1,0:T(8,128)(2,1)} async-done(((bf16[64,8,7168]{2,1,0:T(8,128)(2,1)}), bf16[64,8,7168]{2,1,0:T(8,128)(2,1)}, u32[]{:S(2)}, u32[]{:S(2)}) %all-to-all-start.1) | async-done | bytes 7340064 | tf_op jit(solution)/shard_map/all_to_all | solution.py:78
  194.5 5.8 %all-to-all-start = ((bf16[64,1,8]{2,1,0:T(2,128)(2,1)}), bf16[64,1,8]{2,1,0:T(2,128)(2,1)S(1)}, u32[]{:S(2)}, u32[]{:S(2)}) async-start(bf16[64,1,8]{2,1,0:T(2,128)(2,1)} %copy.22), calls=%async_computation | async-start | bytes 65536 | tf_op jit(solution)/shard_map/all_to_all | solution.py:80
  200.3 5.5 %fusion.7 = f32[512,48]{0,1:T(8,128)S(1)} fusion(bf16[64,8,7168]{2,1,0:T(8,128)(2,1)} %all-to-all-done.1, bf16[1,48,7168]{2,1,0:T(8,128)(2,1)S(1)} %copy-done.4), kind=kOutput, calls=%fused_computation.10 | convolution fusion | flops 352321536 | bytes 8126464 | tf_op jit(solution)/shard_map/dot_general | solution.py:88
  205.8 3.7 %all-to-all-done = bf16[64,1,8]{2,1,0:T(2,128)(2,1)S(1)} async-done(((bf16[64,1,8]{2,1,0:T(2,128)(2,1)}), bf16[64,1,8]{2,1,0:T(2,128)(2,1)S(1)}, u32[]{:S(2)}, u32[]{:S(2)}) %all-to-all-start) | async-done | bytes 1056 | tf_op jit(solution)/shard_map/all_to_all | solution.py:80
  209.5 1.0 broadcast_in_dim.17
  210.5 6.6 %all-to-all-start.2 = ((bf16[64,8,896]{2,1,0:T(8,128)(2,1)}), bf16[64,8,896]{2,1,0:T(8,128)(2,1)S(1)}, u32[]{:S(2)}, u32[]{:S(2)}) async-start(bf16[64,8,896]{2,1,0:T(8,128)(2,1)} %bitcast.11), calls=%async_computation.2 | async-start | bytes 1835008 | tf_op jit(solution)/shard_map/all_to_all | solution.py:79
  217.2 6.0 %multiply_convert_fusion = (bf16[512,48]{0,1:T(8,128)(2,1)S(1)}, f32[512,48]{0,1:T(8,128)}) fusion(f32[512,48]{0,1:T(8,128)S(1)} %fusion.7, bf16[1,48,7168]{2,1,0:T(8,128)(2,1)S(1)} %copy-done.3, bf16[64,8,7168]{2,1,0:T(8,128)(2,1)} %all-to-all-done.1), kind=kOutput, calls=%fused_computation.35 | convolution fusion | flops 352468992 | bytes 8273920 | tf_op jit(solution)/shard_map/dot_general | solution.py:89
  223.3 22.1 %all_gather.3 = bf16[512,384]{0,1:T(8,128)(2,1)S(1)} all-gather(bf16[512,48]{0,1:T(8,128)(2,1)S(1)} %get-tuple-element.5), channel_id=1, replica_groups=mesh['expert'=64,'dp'=8] {'dp'}, dimensions={1}, use_global_device_ids=true | all-gather | bytes 442368 | tf_op jit(solution)/shard_map/all_gather | solution.py:93
  246.1 1.7 fusion.37
  247.8 7.1 %collective-permute-start = (bf16[512,896]{1,0:T(8,128)(2,1)}, bf16[512,896]{1,0:T(8,128)(2,1)}, u32[]{:S(2)}, u32[]{:S(2)}) collective-permute-start(bf16[512,896]{1,0:T(8,128)(2,1)} %get-tuple-element.7), channel_id=1, source_target_pairs={{0,8},{8,0},{16,24},{24,16},{32,40},{40,32},{48,56},{56,48},{64,72... | collective-permute-start | bytes 2752520 | tf_op jit(solution)/shard_map/ppermute | solution.py:17
  255.7 0.8 reshape.73
  257.2 1.5 fusion.10
  258.8 0.9 copy-done.1
  259.7 1.4 convolution_convert_fusion.5
  261.1 2.7 fusion.12
  263.8 31.1 %reduce-scatter.2.cloned.1.call-done = bf16[512,48]{0,1:T(8,128)(2,1)} async-done(((bf16[512,384]{0,1:T(8,128)(2,1)}), bf16[512,48]{0,1:T(8,128)(2,1)}) %reduce-scatter.2.cloned.1.call-update) | async-done | bytes 49168 | tf_op jit(solution)/shard_map/reduce_scatter | solution.py:105
  294.9 5.3 %fusion.2 = bf16[1,48,7168]{2,1,0:T(8,128)(2,1)} fusion(bf16[64,8,7168]{2,1,0:T(8,128)(2,1)} %all-to-all-done.1, bf16[512,48]{0,1:T(8,128)(2,1)} %reduce-scatter.2.cloned.1.call-done, f32[512,48]{0,1:T(8,128)S(1)} %fusion.7), kind=kOutput, calls=%fused_computation.5 | convolution fusion | flops 352837632 | bytes 8175616 | tf_op jit(solution)/shard_map/dot_general | solution.py:114
  300.3 5.3 %fusion.1 = bf16[1,48,7168]{2,1,0:T(8,128)(2,1)} fusion(bf16[64,8,7168]{2,1,0:T(8,128)(2,1)} %all-to-all-done.1, f32[512,48]{0,1:T(8,128)S(1)} %copy-done.5, bf16[512,48]{0,1:T(8,128)(2,1)S(1)} %copy-done.6, f32[512,48]{0,1:T(8,128)S(1)} %fusion.7), kind=kOutput, calls=%fused_computation.4 | convolution fusion | flops 352935936 | bytes 8273920 | tf_op jit(solution)/shard_map/dot_general | solution.py:111
  (37 shorter events, 4.0 us)
Async XLA Ops:
  7.2 239.0 %copy-start = (bf16[1,384,896]{2,1,0:T(8,128)(2,1)S(1)}, bf16[1,384,896]{2,1,0:T(8,128)(2,1)}, u32[]{:S(2)}) copy-start(bf16[1,384,896]{2,1,0:T(8,128)(2,1)} %param.15) | copy-start | bytes 2064388
  16.0 15.1 %copy-start.10 = (bf16[16,8]{0,1:T(8,128)(2,1)S(1)}, bf16[16,8]{0,1:T(8,128)(2,1)}, u32[]{:S(2)}) copy-start(bf16[16,8]{0,1:T(8,128)(2,1)} %param.10) | copy-start | bytes 772
  16.0 16.3 %copy-start.7 = (bf16[16,8,896]{2,1,0:T(8,128)(2,1)S(1)}, bf16[16,8,896]{2,1,0:T(8,128)(2,1)}, u32[]{:S(2)}) copy-start(bf16[16,8,896]{2,1,0:T(8,128)(2,1)} %param.9) | copy-start | bytes 688132
  16.0 184.3 %copy-start.4 = (bf16[1,48,7168]{2,1,0:T(8,128)(2,1)S(1)}, bf16[1,48,7168]{2,1,0:T(8,128)(2,1)}, u32[]{:S(2)}) copy-start(bf16[1,48,7168]{2,1,0:T(8,128)(2,1)} %param.13) | copy-start | bytes 2064388
  16.0 178.5 %all-to-all-start.1 = ((bf16[64,8,7168]{2,1,0:T(8,128)(2,1)}), bf16[64,8,7168]{2,1,0:T(8,128)(2,1)}, u32[]{:S(2)}, u32[]{:S(2)}) async-start(bf16[64,8,7168]{2,1,0:T(8,128)(2,1)} %bitcast.54), calls=%async_computation.1 | async-start | bytes 14680064 | tf_op jit(solution)/shard_map/all_to_all | solution.py:78
  194.5 15.0 %all-to-all-start = ((bf16[64,1,8]{2,1,0:T(2,128)(2,1)}), bf16[64,1,8]{2,1,0:T(2,128)(2,1)S(1)}, u32[]{:S(2)}, u32[]{:S(2)}) async-start(bf16[64,1,8]{2,1,0:T(2,128)(2,1)} %copy.22), calls=%async_computation | async-start | bytes 65536 | tf_op jit(solution)/shard_map/all_to_all | solution.py:80
  200.3 16.9 %copy-start.3 = (bf16[1,48,7168]{2,1,0:T(8,128)(2,1)S(1)}, bf16[1,48,7168]{2,1,0:T(8,128)(2,1)}, u32[]{:S(2)}) copy-start(bf16[1,48,7168]{2,1,0:T(8,128)(2,1)} %param.14) | copy-start | bytes 2064388
  209.5 1.0 copy-start.8
  210.5 46.0 %all-to-all-start.2 = ((bf16[64,8,896]{2,1,0:T(8,128)(2,1)}), bf16[64,8,896]{2,1,0:T(8,128)(2,1)S(1)}, u32[]{:S(2)}, u32[]{:S(2)}) async-start(bf16[64,8,896]{2,1,0:T(8,128)(2,1)} %bitcast.11), calls=%async_computation.2 | async-start | bytes 1835008 | tf_op jit(solution)/shard_map/all_to_all | solution.py:79
  217.2 77.8 %reduce-scatter.2.cloned.1.call-start = ((), (), s32[]{:S(2)}) async-start(), calls=%async_computation.4 | async-start | bytes 442368 | tf_op jit(solution)/shard_map/reduce_scatter | solution.py:105
  223.3 31.7 %copy-start.9 = (bf16[64,1,8]{2,1,0:T(2,128)(2,1)S(1)}, bf16[64,1,8]{2,1,0:T(2,128)(2,1)}, u32[]{:S(2)}) copy-start(bf16[64,1,8]{2,1,0:T(2,128)(2,1)} %copy-done.8) | copy-start | bytes 3076
  245.4 0.7 copy-start.2
  247.8 9.4 %collective-permute-start = (bf16[512,896]{1,0:T(8,128)(2,1)}, bf16[512,896]{1,0:T(8,128)(2,1)}, u32[]{:S(2)}, u32[]{:S(2)}) collective-permute-start(bf16[512,896]{1,0:T(8,128)(2,1)} %get-tuple-element.7), channel_id=1, source_target_pairs={{0,8},{8,0},{16,24},{24,16},{32,40},{40,32},{48,56},{56,48},{64,72... | collective-permute-start | bytes 2752520 | tf_op jit(solution)/shard_map/ppermute | solution.py:17
  258.7 0.9 copy-start.1
  263.8 36.5 %copy-start.5 = (f32[512,48]{0,1:T(8,128)S(1)}, f32[512,48]{0,1:T(8,128)}, u32[]{:S(2)}) copy-start(f32[512,48]{0,1:T(8,128)} %get-tuple-element.6) | copy-start | bytes 294916
  294.9 5.3 %copy-start.6 = (bf16[512,48]{0,1:T(8,128)(2,1)S(1)}, bf16[512,48]{0,1:T(8,128)(2,1)}, u32[]{:S(2)}) copy-start(bf16[512,48]{0,1:T(8,128)(2,1)} %reduce-scatter.2.cloned.1.call-done) | copy-start | bytes 147460
Sparse Core Ops, SparseCore 0:
  261.2 33.6 reduce-scatter.1
where the time goes:
time: 317 us; the launch traced here: 312 us
  waiting for transfers between devices  197 us (62%)
  starting transfers between devices  34.7 us (11%)
  matrix products  30.7 us (10%)
  blocking collectives  22.1 us (7%)
  between operations  14.2 us (4%)
  local copies, waits for them, and re-layouts  9.3 us (3%)
  other arithmetic  4.08 us (1%)
    all_to_all x1, waiting for transfers between devices, body(): lax.all_to_all(outgoing[0], 'expert', split_axis=0, concat_axis=0, tiled=...  162 us
    reduce_scatter x1, waiting for transfers between devices, body(): lax.psum_scatter(back_terms.astype(jnp.bfloat16), 'dp', scatter_dimension...  31.1 us
    all_gather x1, blocking collectives, body(): hidden_half = lax.all_gather(hidden, 'dp', axis=1, tiled=True)  22.1 us
    all_to_all x1, starting transfers between devices, body(): lax.all_to_all(outgoing[0], 'expert', split_axis=0, concat_axis=0, tiled=...  15.1 us
    ppermute x1, starting transfers between devices, partner(): return lax.ppermute(block, axis, route)  7.13 us
    all_to_all x1, starting transfers between devices, body(): lax.all_to_all(outgoing[1], 'expert', split_axis=0, concat_axis=0, tiled=...  6.64 us
  transfers between devices with their start and end apart: 5, of which 4 were waited for; matrix products, arithmetic and copies ran while one was open for 6% of the time, Pallas kernels for 0%

commit v1 on v0

v1 whole, which is shorter than its diff:
```python
import functools
import jax
import jax.numpy as jnp
from jax import lax
from jax.experimental import pallas as pl
from jax.experimental.pallas import tpu as pltpu
from jax.sharding import PartitionSpec as P

BF = jnp.bfloat16
F32 = jnp.float32
XS = 4
NT_DIMS = (((1,), (1,)), ((), ()))
TN_DIMS = (((0,), (0,)), ((), ()))


def hot(cond):
    return jnp.where(cond, 1.0, 0.0).astype(BF)


def iota(shape, dim):
    return lax.broadcasted_iota(jnp.int32, shape, dim)


def target_width(feature):
    return -(-(feature + 128) // 256) * 128


def pack_kernel(tokens, teacher, weight, routes, twin_col, twin_row, pay_rows, pay_target):
    block, topk = routes.shape
    pairs = block * topk
    teachers = twin_col.shape[0]
    cap = 2 * pairs // teachers
    group = 2 * cap
    feature = teacher.shape[2]
    width = target_width(feature)
    rows = pay_rows.shape[0] * pay_rows.shape[1]
    cls = lax.rem(lax.axis_index("dp"), 4)

    token_of = hot(iota((pairs, block), 0) // topk == iota((pairs, block), 1))
    token_of_t = hot(iota((block, pairs), 1) // topk == iota((block, pairs), 0))
    place_col = iota((pairs, topk), 0) % topk == iota((pairs, topk), 1)
    place_row = iota((topk, pairs), 1) % topk == iota((topk, pairs), 0)
    named = routes[...].astype(F32).astype(BF)
    teach_col = jnp.sum(
        jnp.where(place_col, jnp.dot(token_of, named, preferred_element_type=F32), 0.0),
        axis=1, keepdims=True)
    teach_row = jnp.sum(
        jnp.where(place_row, lax.dot_general(named, token_of_t, TN_DIMS, preferred_element_type=F32), 0.0),
        axis=0, keepdims=True)
    weight_col = jnp.sum(
        jnp.where(place_col, jnp.dot(token_of, weight[...], preferred_element_type=F32), 0.0),
        axis=1, keepdims=True)
    earlier = iota((pairs, pairs), 0) < iota((pairs, pairs), 1)
    rank_row = jnp.sum(
        jnp.where((teach_col == teach_row) & earlier, 1.0, 0.0), axis=0, keepdims=True)
    twins = twin_col[...] == twin_row[...]
    before = iota((teachers, teachers), 1) < iota((teachers, teachers), 0)
    twin_of = jnp.sum(jnp.where(twins & before, 1.0, 0.0), axis=1, keepdims=True)
    first_slot = twin_col[...].astype(F32) * float(group) + twin_of * float(cap)
    teacher_hot = iota((teachers, pairs), 0).astype(F32) == teach_row
    slot_row = rank_row + jnp.sum(jnp.where(teacher_hot, first_slot, 0.0), axis=0, keepdims=True)

    row_ids = iota((rows, pairs), 0)
    slot_of = (row_ids // (2 * group)) * group + row_ids % group
    half_of = (row_ids // group) % 2
    filled = slot_of.astype(F32) == slot_row
    put_low = hot(filled & (half_of == 0))
    put_high = hot(filled & (half_of == 1))

    spread = hot(iota((pairs, 2 * block), 0) // topk == iota((pairs, 2 * block), 1) % block)
    pick = jnp.dot(hot(filled), spread, preferred_element_type=F32)
    pick_half = iota((rows, 2 * block), 1) // block == (iota((rows, 2 * block), 0) // group) % 2
    pick = jnp.where(pick_half, pick, 0.0).astype(BF)
    low = tokens[:, pl.ds(pl.multiple_of(cls * feature, 128), feature)]
    high = tokens[:, pl.ds(pl.multiple_of((cls + 4) * feature, 128), feature)]
    both = jnp.concatenate([low, high], axis=0)
    sent = jnp.dot(pick, both, preferred_element_type=F32).astype(BF)
    pay_rows[...] = sent.reshape(pay_rows.shape)

    target = teacher[...].astype(F32).reshape(pairs, feature).astype(BF)
    spread_weight = jnp.broadcast_to(weight_col, (pairs, 128)).astype(BF)
    tail = jnp.concatenate([target[:, width:], spread_weight], axis=1)
    sent = jnp.dot(put_low, target[:, :width], preferred_element_type=F32) + jnp.dot(
        put_high, tail, preferred_element_type=F32)
    pay_target[...] = sent.astype(BF).reshape(pay_target.shape)


def main_kernel(
    pay_rows, pay_target, gate, up, down,
    grad_gate, grad_up, grad_down,
    rows, target, weights, weights_down, pre, slots_pre, hidden, err, back_out, back_in,
    down_own, down_out, down_in, expand, own, gate_out, gate_in,
    w_recv, w_local, w_send, rows_recv, rows_send, target_recv, target_send,
    left_recv, right_recv, fwd_left_recv, fwd_right_recv, ring_send,
    hid_send, hid_recv, back_send, back_recv, down_send, down_recv, gate_send, gate_recv,
):
    chips = pay_rows.shape[0]
    line = chips // XS
    height = pay_rows.shape[1]
    group = height // 2
    feature = pay_rows.shape[2]
    width = pay_target.shape[2]
    tail = feature - width
    units = gate.shape[0]
    count_y = down.shape[0]
    slots = chips * group
    me = lax.axis_index("expert")
    y = lax.axis_index("dp")
    core = lax.rem(me, 2)
    other = 1 - core
    chip = me // 2
    x = chip // line
    z = lax.rem(chip, line)
    sibling = (chip * 2 + other, y)
    right_y = lax.rem(y + 1, count_y)
    left_y = lax.rem(y + count_y - 1, count_y)
    right = (me, right_y)
    left = (me, left_y)

    def peer(step):
        dx = step // line
        to = lax.rem(x + XS - dx, XS) * line + lax.rem(z + step, line)
        return dx, to

    def remote(src, dst, send_sem, recv_sem, device):
        return pltpu.make_async_remote_copy(
            src_ref=src, dst_ref=dst, send_sem=send_sem, recv_sem=recv_sem,
            device_id=device, device_id_type=pl.DeviceIdType.MESH)

    def await_bytes(ref, sem):
        pltpu.make_async_copy(ref, ref, sem).wait()

    barrier = pltpu.get_barrier_semaphore()
    pl.semaphore_signal(barrier, inc=1, device_id=sibling, device_id_type=pl.DeviceIdType.MESH)

    def greet_chip(step, carry):
        _, to = peer(step)
        pl.semaphore_signal(
            barrier, inc=1, device_id=(to * 2 + core, y), device_id_type=pl.DeviceIdType.MESH)
        return carry

    def greet_y(step, carry):
        pl.semaphore_signal(
            barrier, inc=1, device_id=(me, lax.rem(y + step, count_y)),
            device_id_type=pl.DeviceIdType.MESH)
        return carry

    lax.fori_loop(1, chips, greet_chip, 0)
    lax.fori_loop(1, count_y, greet_y, 0)

    own_copies = [
        pltpu.make_async_copy(gate, weights.at[core, 0], w_local.at[0]),
        pltpu.make_async_copy(up, weights.at[core, 1], w_local.at[1]),
        pltpu.make_async_copy(down, weights_down.at[:, core], w_local.at[2]),
        pltpu.make_async_copy(pay_rows.at[chip], rows.at[0, chip], rows_recv.at[0]),
        pltpu.make_async_copy(pay_target.at[chip], target.at[chip], target_recv),
    ]
    for copy in own_copies:
        copy.start()
    pl.semaphore_wait(barrier, chips - 1 + count_y - 1 + 1)

    def send_rows(step, carry):
        dx, to = peer(step)
        remote(pay_rows.at[to], rows.at[0, chip], rows_send, rows_recv.at[dx], (to * 2 + core, y)).start()
        return carry

    def send_target(step, carry):
        _, to = peer(step)
        remote(pay_target.at[to], target.at[chip], target_send, target_recv, (to * 2 + core, y)).start()
        return carry

    lax.fori_loop(1, chips, send_rows, 0)
    weight_copies = [
        remote(gate, weights.at[core, 0], w_send.at[0], w_recv.at[0], sibling),
        remote(up, weights.at[core, 1], w_send.at[1], w_recv.at[1], sibling),
        remote(down, weights_down.at[:, core], w_send.at[2], w_recv.at[2], sibling),
    ]
    for copy in weight_copies:
        copy.start()
    lax.fori_loop(1, chips, send_target, 0)

    def chunk_at(step):
        return lax.rem(x + step, XS) * line

    def send_own(step):
        at = pl.ds(chunk_at(step), line)
        await_bytes(rows.at[0, at], rows_recv.at[step])
        remote(rows.at[0, at], rows.at[3, at], ring_send.at[0], left_recv.at[step], right).start()
        remote(rows.at[0, at], rows.at[1, at], ring_send.at[1], right_recv.at[step], left).start()

    def forward(step):
        at = pl.ds(chunk_at(step), line)
        first = pl.ds(chunk_at(step), line // 2)
        last = pl.ds(chunk_at(step) + line // 2, line // 2)
        await_bytes(rows.at[3, at], left_recv.at[step])
        remote(rows.at[3, first], rows.at[2, first], ring_send.at[2], fwd_left_recv.at[step], right).start()
        await_bytes(rows.at[1, at], right_recv.at[step])
        remote(rows.at[1, last], rows.at[2, last], ring_send.at[3], fwd_right_recv.at[step], left).start()

    def slice_of(cls):
        return pl.ds(pl.multiple_of(cls * feature, 128), feature)

    def project(step):
        at = chunk_at(step)
        await_bytes(rows.at[2, pl.ds(at, line // 2)], fwd_left_recv.at[step])
        await_bytes(rows.at[2, pl.ds(at + line // 2, line // 2)], fwd_right_recv.at[step])
        pre[...] = jnp.zeros_like(pre)

        def add(rel, carry):
            cls = lax.rem(y + rel, 4)
            part = rows[rel, pl.ds(at, line)].reshape(line * height, feature)
            for half in range(2):
                w = weights[:, :, :, slice_of(cls + 4 * half)].reshape(4 * units, feature)
                pre[half] += lax.dot_general(part, w, NT_DIMS, preferred_element_type=F32)
            return carry

        lax.fori_loop(0, 4, add, 0)
        low = pre[0].reshape(line, height, 4 * units)[:, :group]
        high = pre[1].reshape(line, height, 4 * units)[:, group:]
        first = pl.multiple_of(at * group, group)
        slots_pre[pl.ds(first, line * group), : 4 * units] = (low + high).reshape(line * group, 4 * units)

    slots_pre[...] = jnp.zeros_like(slots_pre)
    send_own(0)
    for copy in own_copies[:3]:
        copy.wait()
    for copy in weight_copies:
        copy.wait()
    for step in range(XS):
        if step + 1 < XS:
            send_own(step + 1)
        forward(step)
        if step > 0:
            project(step - 1)
    project(XS - 1)

    gates = slots_pre[...].T[: 4 * units].reshape(2, 2, units, slots)
    gate_pre = gates[:, 0].reshape(2 * units, slots)
    up_pre = gates[:, 1].reshape(2 * units, slots)
    sig = 1.0 / (1.0 + jnp.exp(-gate_pre))
    silu = gate_pre * sig
    hidden[y] = (silu * up_pre).astype(BF)

    def send_hidden(step, carry):
        to = lax.rem(y + step, count_y)
        remote(hidden.at[y], hidden.at[y], hid_send, hid_recv, (me, to)).start()
        return carry

    lax.fori_loop(1, count_y, send_hidden, 0)
    await_bytes(target, target_recv)
    await_bytes(hidden.at[pl.ds(0, count_y - 1)], hid_recv)

    all_hidden = hidden[...].reshape(count_y * 2 * units, slots)
    all_down = weights_down[...].reshape(count_y * 2 * units, feature)
    out = lax.dot_general(all_hidden, all_down, TN_DIMS, preferred_element_type=F32)
    arrived = target[...].astype(F32)
    goal_low = arrived[:, :group].reshape(slots, width)
    goal_high = arrived[:, group:].reshape(slots, width)
    slot_weight = goal_high[:, tail : tail + 1]
    err[:, :width] = (slot_weight * (out[:, :width] - goal_low)).astype(BF)
    err[:, width:] = (slot_weight * (out[:, width:] - goal_high[:, :tail])).astype(BF)

    def send_back(step, carry):
        to = lax.rem(y + step, count_y)
        w = weights_down[to].reshape(2 * units, feature)
        back_out[to] = lax.dot_general(w, err[...], NT_DIMS, preferred_element_type=F32).astype(BF)

        @pl.when(step < count_y)
        def _():
            remote(back_out.at[to], back_in.at[y], back_send, back_recv, (me, to)).start()
        return carry

    lax.fori_loop(1, count_y + 1, send_back, 0)

    def down_part(part, carry):
        term = jnp.dot(hidden[part], err[...], preferred_element_type=F32)
        down_own[part] = term.reshape(2, units, feature)
        down_out[part] = down_own[part, other].astype(BF)
        return carry

    lax.fori_loop(0, count_y, down_part, 0)
    down_copy = remote(down_out, down_in, down_send, down_recv, sibling)
    down_copy.start()

    await_bytes(back_in.at[pl.ds(0, count_y - 1)], back_recv)
    back_hidden = back_out[y].astype(F32)

    def add_back(step, total):
        return total + back_in[lax.rem(y + step, count_y)].astype(F32)

    back_hidden = lax.fori_loop(1, count_y, add_back, back_hidden)
    slope = sig * (1.0 + gate_pre * (1.0 - sig))
    back_gate = (back_hidden * up_pre * slope).astype(BF).reshape(2, 1, units, slots)
    back_up = (back_hidden * silu).astype(BF).reshape(2, 1, units, slots)
    backs = jnp.concatenate([back_gate, back_up], axis=1).reshape(4 * units, slots)
    wide = (slots, chips * height)
    for half in range(2):
        slot_id, lane = iota(wide, 0), iota(wide, 1)
        match = (lane // height == slot_id // group) & (lane % height == slot_id % group + group * half)
        expand[half] = jnp.dot(backs, hot(match), preferred_element_type=F32).astype(BF)

    def class_part(rel, carry):
        cls = lax.rem(y + rel, 4)
        lhs = expand[...].reshape(8 * units, chips * height)
        part = rows[rel].reshape(chips * height, feature)
        own[rel] = jnp.dot(lhs, part, preferred_element_type=F32).reshape(2, 2, 2 * units, feature)
        gate_out[cls] = own[rel, :, other].astype(BF)
        remote(gate_out.at[cls], gate_in.at[cls], gate_send, gate_recv.at[rel], sibling).start()
        return carry

    lax.fori_loop(0, 4, class_part, 0)

    down_copy.wait()

    def down_sum(part, carry):
        grad_down[part] = (down_own[part, core] + down_in[part].astype(F32)).astype(BF)
        return carry

    lax.fori_loop(0, count_y, down_sum, 0)

    def gate_sum(rel, carry):
        cls = lax.rem(y + rel, 4)
        await_bytes(gate_in.at[cls], gate_recv.at[rel])
        for half in range(2):
            total = (own[rel, half, core] + gate_in[cls, half].astype(F32)).astype(BF)
            grad_gate[:, slice_of(cls + 4 * half)] = total[:units]
            grad_up[:, slice_of(cls + 4 * half)] = total[units:]
        return carry

    lax.fori_loop(0, 4, gate_sum, 0)

    await_bytes(pay_rows.at[pl.ds(0, chips - 1)], rows_send)
    await_bytes(pay_target.at[pl.ds(0, chips - 1)], target_send)
    await_bytes(rows.at[0], ring_send.at[0])
    await_bytes(rows.at[0], ring_send.at[1])
    await_bytes(rows.at[0, pl.ds(0, chips // 2)], ring_send.at[2])
    await_bytes(rows.at[0, pl.ds(0, chips // 2)], ring_send.at[3])
    await_bytes(hidden.at[pl.ds(0, count_y - 1)], hid_send)
    await_bytes(back_out.at[pl.ds(0, count_y - 1)], back_send)
    await_bytes(gate_out, gate_send)


def body(
    tokens, teacher_out, route_weight, routes, twin_map, student_gate, student_up, student_down
):
    block, topk = routes.shape
    teachers = twin_map.shape[0]
    chips = teachers // 2
    cap = 2 * block * topk // teachers
    height = 4 * cap
    feature = teacher_out.shape[2]
    width = target_width(feature)
    model = tokens.shape[1]
    units = student_gate.shape[1]
    count_y = model // feature
    slots = chips * 2 * cap
    vmem = pl.BlockSpec(memory_space=pltpu.VMEM)
    anywhere = pl.BlockSpec(memory_space=pl.ANY)
    pay_rows, pay_target = pl.pallas_call(
        pack_kernel,
        out_shape=(
            jax.ShapeDtypeStruct((chips, height, feature), BF),
            jax.ShapeDtypeStruct((chips, height, width), BF),
        ),
        in_specs=[vmem] * 6,
        out_specs=(vmem, vmem),
        compiler_params=pltpu.CompilerParams(vmem_limit_bytes=48 * 1024 * 1024),
    )(
        tokens, teacher_out, route_weight, routes,
        twin_map.reshape(teachers, 1), twin_map.reshape(1, teachers),
    )
    dma = pltpu.SemaphoreType.DMA
    grads = pl.pallas_call(
        main_kernel,
        out_shape=(
            jax.ShapeDtypeStruct((units, model), BF),
            jax.ShapeDtypeStruct((units, model), BF),
            jax.ShapeDtypeStruct((count_y, units, feature), BF),
        ),
        in_specs=[anywhere] * 5,
        out_specs=(vmem, vmem, vmem),
        scratch_shapes=[
            pltpu.VMEM((4, chips, height, feature), BF),
            pltpu.VMEM((chips, height, width), BF),
            pltpu.VMEM((2, 2, units, model), BF),
            pltpu.VMEM((count_y, 2, units, feature), BF),
            pltpu.VMEM((2, chips // XS * height, 4 * units), F32),
            pltpu.VMEM((slots, -(-4 * units // 128) * 128), F32),
            pltpu.VMEM((count_y, 2 * units, slots), BF),
            pltpu.VMEM((slots, feature), BF),
            pltpu.VMEM((count_y, 2 * units, slots), BF),
            pltpu.VMEM((count_y, 2 * units, slots), BF),
            pltpu.VMEM((count_y, 2, units, feature), F32),
            pltpu.VMEM((count_y, units, feature), BF),
            pltpu.VMEM((count_y, units, feature), BF),
            pltpu.VMEM((2, 4 * units, chips * height), BF),
            pltpu.VMEM((4, 2, 2, 2 * units, feature), F32),
            pltpu.VMEM((4, 2, 2 * units, feature), BF),
            pltpu.VMEM((4, 2, 2 * units, feature), BF),
            dma((3,)), dma((3,)), dma((3,)),
            dma((XS,)), dma, dma, dma,
            dma((XS,)), dma((XS,)), dma((XS,)), dma((XS,)), dma((4,)),
            dma, dma, dma, dma, dma, dma, dma, dma((4,)),
        ],
        compiler_params=pltpu.CompilerParams(
            collective_id=0, has_side_effects=True, vmem_limit_bytes=56 * 1024 * 1024),
    )(
        pay_rows, pay_target, student_gate[0], student_up[0],
        student_down[0].reshape(count_y, units, feature),
    )
    return (
        grads[0][None], grads[1][None], grads[2].reshape(1, count_y * units, feature))


def solution(mesh):
    placed = (
        P("expert", None),
        P("expert", None, "dp"),
        P("expert", None),
        P("expert", None),
        P(),
        P("expert", "dp", None),
        P("expert", "dp", None),
        P("expert", None, "dp"),
    )
    return jax.shard_map(
        body,
        mesh=mesh,
        in_specs=placed,
        out_specs=(P("expert", "dp", None), P("expert", "dp", None), P("expert", None, "dp")),
        check_vma=False,
    )
```

time: 317 us -> 96.5 us (0.30); the launches traced: 312 us -> 95.3 us
  waiting for transfers between devices: 197 us -> 0 us
  Pallas kernels: 0 us -> 85.2 us
  starting transfers between devices: 34.7 us -> 0 us
  matrix products: 30.7 us -> 0 us
  blocking collectives: 22.1 us -> 0 us
  between operations: 14.2 us -> 0.69 us
  other arithmetic: 4.08 us -> 0 us
    all_to_all x3 -> x0, waiting for transfers between devices: 165 us -> none  [the longest x1 162 us: body(): lax.all_to_all(outgoing[0], 'expert', split_axis=0, concat_axis=0, tiled=...]
    pallas_call x0 -> x2, Pallas kernels: none -> 85.2 us  [the longest x1 84.2 us: body(): pl.pallas_call(main_kernel, out_shape=(jax.ShapeDtypeStruct((units, model...]
    reduce_scatter x1 -> x0, waiting for transfers between devices: 31.1 us -> none  [body(): lax.psum_scatter(back_terms.astype(jnp.bfloat16), 'dp', scatter_dimension...]
    dot_general x10 -> x0, matrix products: 30.7 us -> none  [the longest x1 6.05 us: body(): lax.dot_general(slot_rows, w_up, last_dims, preferred_element_type=jnp.fl...]
    all_to_all x3 -> x0, starting transfers between devices: 27.6 us -> none  [the longest x1 15.1 us: body(): lax.all_to_all(outgoing[0], 'expert', split_axis=0, concat_axis=0, tiled=...]
    all_gather x1 -> x0, blocking collectives: 22.1 us -> none  [body(): hidden_half = lax.all_gather(hidden, 'dp', axis=1, tiled=True)]
    ppermute x1 -> x0, starting transfers between devices: 7.13 us -> none  [partner(): return lax.ppermute(block, axis, route)]
    unnamed x24 -> x23, local copies, waits for them, and re-layouts: 2.62 us -> 9.26 us
  transfers between devices with their start and end apart: 5 -> 0, of which waited for: 4 -> 0; matrix products, arithmetic and copies ran while one was open for 6% -> 0% of each run, Pallas kernels for 0% -> 0%
where the time goes in v1:
time: 96.5 us; the launch traced here: 95.3 us
  Pallas kernels  85.2 us (88%)
  local copies, waits for them, and re-layouts  9.35 us (10%)
    pallas_call x1, Pallas kernels, body(): pl.pallas_call(main_kernel, out_shape=(jax.ShapeDtypeStruct((units, model...  84.2 us
    unnamed x23, local copies, waits for them, and re-layouts  9.26 us

profile of v1, /device:TPU:1, one launch (start us, length us, event | category | flops | bytes accessed | tf_op | source)
XLA Modules:
  0.0 95.3 jit_solution(14969918932618943588)
XLA Ops:
  0.6 0.0 copy-start.8
  0.6 0.0 copy-start.7
  0.7 0.7 copy-done.8
  1.3 0.1 copy.11.weight
  1.4 0.0 copy-done.7
  1.4 0.1 copy.12.routes
  1.5 0.6 copy-done.4
  2.1 0.1 copy.13.twin_col
  2.2 0.0 copy-start.2
  2.2 0.9 copy-done.2
  3.1 0.0 copy-start.3
  3.1 0.9 copy-done.3
  4.0 1.0 %shard_map.103 = (bf16[32,16,896]{2,1,0:T(8,128)(2,1)S(1)}, bf16[32,16,512]{2,1,0:T(8,128)(2,1)S(1)}) custom-call(bf16[16,7168]{1,0:T(8,128)(2,1)S(1)} %copy-done.2, bf16[16,8,896]{2,1,0:T(8,128)(2,1)S(1)} %copy-done.3, bf16[16,8]{1,0:T(8,128)(2,1)S(1)} %copy.11.weight, s32[16,8]{1,0:T(8,128)S(1)} %copy.12.routes, s32[64,1]{1,0:T(8,128)S(1)} %copy.13.twin_col, ...), custom_call_target="tpu_custom_call" | custom-call | tf_op jit(solution)/shard_map/pallas_call | solution.py:359
  5.1 0.0 copy-start
  5.1 0.9 copy-done
  6.0 0.0 copy-start.1
  6.0 0.8 copy-done.1
  6.8 84.2 %shard_map.104 = (bf16[48,7168]{1,0:T(8,128)(2,1)}, bf16[48,7168]{1,0:T(8,128)(2,1)}, bf16[8,48,896]{2,1,0:T(8,128)(2,1)}) custom-call(bf16[32,16,896]{2,1,0:T(8,128)(2,1)} %copy-done, bf16[32,16,512]{2,1,0:T(8,128)(2,1)} %copy-done.1, bf16[48,7168]{1,0:T(8,128)(2,1)} %bitcast.10, bf16[48,7168]{1,0:T(8,128)(2,1)} %bitcast.11, bf16[8,48,896]{2,1,0:T(8,128)(2,1)} %bitcast.12), custom_call_target="tpu_custom_call" | custom-call | tf_op jit(solution)/shard_map/pallas_call | solution.py:373
  91.0 0.0 copy-start.6
  91.0 2.1 %copy.17 = bf16[1,48,7168]{2,1,0:T(8,128)(2,1)} copy(bf16[1,48,7168]{2,1,0:T(8,128)(2,1)} %bitcast.15) | data formatting | bytes 1376256
  93.1 0.0 copy-done.6
  93.1 0.8 copy.18
  93.9 0.5 copy-done.5
  94.4 0.8 copy.19
  (2 shorter events, 0.0 us)
Async XLA Ops:
  0.6 0.7 copy-start.8
  0.6 0.8 copy-start.7
  1.4 0.7 copy-start.4
  2.2 0.9 copy-start.2
  3.1 0.9 copy-start.3
  5.1 0.9 copy-start
  6.0 0.8 copy-start.1
  91.0 2.1 %copy-start.6 = (bf16[48,7168]{1,0:T(8,128)(2,1)S(1)}, bf16[48,7168]{1,0:T(8,128)(2,1)}, u32[]{:S(2)}) copy-start(bf16[48,7168]{1,0:T(8,128)(2,1)} %get-tuple-element.11) | copy-start | bytes 2064388
  93.1 1.3 %copy-start.5 = (bf16[8,48,896]{2,1,0:T(8,128)(2,1)S(1)}, bf16[8,48,896]{2,1,0:T(8,128)(2,1)}, u32[]{:S(2)}) copy-start(bf16[8,48,896]{2,1,0:T(8,128)(2,1)} %get-tuple-element.12) | copy-start | bytes 2064388

commit v2 on v1

v2 whole, which is shorter than its diff:
```python
import functools
import jax
import jax.numpy as jnp
from jax import lax
from jax.experimental import pallas as pl
from jax.experimental.pallas import tpu as pltpu
from jax.sharding import PartitionSpec as P

BF = jnp.bfloat16
F32 = jnp.float32
XS = 4
NT_DIMS = (((1,), (1,)), ((), ()))
TN_DIMS = (((0,), (0,)), ((), ()))


def hot(cond):
    return jnp.where(cond, 1.0, 0.0).astype(BF)


def iota(shape, dim):
    return lax.broadcasted_iota(jnp.int32, shape, dim)


def target_width(feature):
    return -(-(feature + 128) // 256) * 128


def ring_chunks(chips):
    halves = []
    for start in (0, chips // 2):
        end = start + chips // 2
        chunks = [(start, XS)]
        while sum(chunks[-1]) < end:
            first = sum(chunks[-1])
            chunks.append((first, min(2 * XS, end - first)))
        halves.append(chunks)
    return halves


def pack(tokens, teacher, weight, routes, twin, pay_rows, pay_target):
    topk, block = routes.shape
    pairs = block * topk
    teachers = twin.shape[1]
    cap = 2 * pairs // teachers
    group = 2 * cap
    width = pay_target.shape[2]
    rows = pay_rows.shape[0] * pay_rows.shape[1]

    token_of = hot(iota((pairs, block), 0) // topk == iota((pairs, block), 1))
    token_of_t = hot(iota((block, pairs), 1) // topk == iota((block, pairs), 0))
    place_col = iota((pairs, topk), 0) % topk == iota((pairs, topk), 1)
    place_row = iota((topk, pairs), 1) % topk == iota((topk, pairs), 0)
    named = routes[...].astype(F32).astype(BF)
    teach_col = jnp.sum(
        jnp.where(place_col, lax.dot_general(token_of, named, NT_DIMS, preferred_element_type=F32), 0.0),
        axis=1, keepdims=True)
    teach_row = jnp.sum(
        jnp.where(place_row, jnp.dot(named, token_of_t, preferred_element_type=F32), 0.0),
        axis=0, keepdims=True)
    weight_col = jnp.sum(
        jnp.where(
            place_col, lax.dot_general(token_of, weight[...], NT_DIMS, preferred_element_type=F32), 0.0),
        axis=1, keepdims=True)
    earlier = iota((pairs, pairs), 0) < iota((pairs, pairs), 1)
    rank_row = jnp.sum(
        jnp.where((teach_col == teach_row) & earlier, 1.0, 0.0), axis=0, keepdims=True)
    twin_row = jnp.broadcast_to(twin[...].astype(F32), (teachers, teachers))
    same = iota((teachers, teachers), 0) == iota((teachers, teachers), 1)
    twin_col = jnp.sum(jnp.where(same, twin_row, 0.0), axis=1, keepdims=True)
    before = iota((teachers, teachers), 1) < iota((teachers, teachers), 0)
    twin_of = jnp.sum(
        jnp.where((twin_col == twin_row) & before, 1.0, 0.0), axis=1, keepdims=True)
    first_slot = twin_col * float(group) + twin_of * float(cap)
    teacher_hot = iota((teachers, pairs), 0).astype(F32) == teach_row
    slot_row = rank_row + jnp.sum(jnp.where(teacher_hot, first_slot, 0.0), axis=0, keepdims=True)

    row_ids = iota((rows, pairs), 0)
    slot_of = (row_ids // (2 * group)) * group + row_ids % group
    half_of = (row_ids // group) % 2
    filled = slot_of.astype(F32) == slot_row
    put_low = hot(filled & (half_of == 0))
    put_high = hot(filled & (half_of == 1))

    spread = hot(iota((pairs, 2 * block), 0) // topk == iota((pairs, 2 * block), 1) % block)
    pick = jnp.dot(hot(filled), spread, preferred_element_type=F32)
    pick_half = iota((rows, 2 * block), 1) // block == (iota((rows, 2 * block), 0) // group) % 2
    pick = jnp.where(pick_half, pick, 0.0).astype(BF)
    sent = jnp.dot(pick, tokens[...], preferred_element_type=F32).astype(BF)
    pay_rows[...] = sent.reshape(pay_rows.shape)

    spread_weight = jnp.broadcast_to(weight_col, (pairs, 128)).astype(BF)
    tail = jnp.concatenate([teacher[:, width:], spread_weight], axis=1)
    sent = jnp.dot(put_low, teacher[:, :width], preferred_element_type=F32) + jnp.dot(
        put_high, tail, preferred_element_type=F32)
    pay_target[...] = sent.astype(BF).reshape(pay_target.shape)


def main_kernel(
    tokens, teacher, weight, routes, twin, gate, up, down,
    gate_own, gate_in, down_kept, down_in,
    own_tokens, own_teacher, own_weight, own_routes, own_twin, pay_rows, pay_target, rows, target, weights, weights_down, pre, slots_pre, hidden, err, back_out, back_in,
    down_out, down_part_both, expand, kept, gate_out, gate_both,
    in_local, w_recv, w_local, w_send, rows_recv, rows_send, target_recv, target_send,
    left_recv, right_recv, fwd_left_recv, fwd_right_recv, ring_send,
    hid_send, hid_recv, back_send, back_recv, down_send, down_recv, gate_send, gate_recv,
):
    chips = pay_rows.shape[0]
    line = chips // XS
    height = pay_rows.shape[1]
    group = height // 2
    feature = pay_rows.shape[2]
    width = pay_target.shape[2]
    tail = feature - width
    units = gate.shape[0]
    count_y = down.shape[0]
    slots = chips * group
    block = tokens.shape[0]
    me = lax.axis_index("expert")
    y = lax.axis_index("dp")
    core = lax.rem(me, 2)
    other = 1 - core
    chip = me // 2
    x = chip // line
    z = lax.rem(chip, line)
    sibling = (chip * 2 + other, y)
    right_y = lax.rem(y + 1, count_y)
    left_y = lax.rem(y + count_y - 1, count_y)
    right = (me, right_y)
    left = (me, left_y)

    def peer(step):
        dx = lax.rem(step, XS)
        turn = step // XS
        dz = jnp.where(lax.rem(turn, 2) == 1, (turn + 1) // 2, line - turn // 2)
        return lax.rem(x + XS - dx, XS) * line + lax.rem(z + 2 * line - dz, line)

    halves = ring_chunks(chips)
    chunks = halves[0] + halves[1]
    part_chips = chips // 2
    part_slots = slots // 2

    def slice_of(cls):
        return pl.ds(pl.multiple_of(cls * feature, 128), feature)

    def remote(src, dst, send_sem, recv_sem, device):
        return pltpu.make_async_remote_copy(
            src_ref=src, dst_ref=dst, send_sem=send_sem, recv_sem=recv_sem,
            device_id=device, device_id_type=pl.DeviceIdType.MESH)

    def await_bytes(ref, sem):
        pltpu.make_async_copy(ref, ref, sem).wait()

    barrier = pltpu.get_barrier_semaphore()
    pl.semaphore_signal(barrier, inc=1, device_id=sibling, device_id_type=pl.DeviceIdType.MESH)

    to_x = [lax.rem(x + XS - dx, XS) * line for dx in range(XS)]
    to_z = []
    for turn in range(line):
        dz = (turn + 1) // 2 if turn % 2 else (line - turn // 2) % line
        to_z.append(lax.rem(z + line - dz, line))

    for step in range(1, chips):
        pl.semaphore_signal(
            barrier, inc=1, device_id=((to_x[step % XS] + to_z[step // XS]) * 2 + core, y), device_id_type=pl.DeviceIdType.MESH)
    for step in range(1, count_y):
        pl.semaphore_signal(
            barrier, inc=1, device_id=(me, lax.rem(y + step, count_y)),
            device_id_type=pl.DeviceIdType.MESH)

    cls = lax.rem(y, 4)
    in_copies = [
        pltpu.make_async_copy(tokens.at[:, slice_of(cls)], own_tokens.at[pl.ds(0, block)], in_local.at[0]),
        pltpu.make_async_copy(
            tokens.at[:, slice_of(cls + 4)], own_tokens.at[pl.ds(block, block)], in_local.at[1]),
        pltpu.make_async_copy(teacher, own_teacher, in_local.at[2]),
        pltpu.make_async_copy(weight, own_weight, in_local.at[3]),
        pltpu.make_async_copy(routes, own_routes, in_local.at[4]),
        pltpu.make_async_copy(twin, own_twin, in_local.at[5]),
    ]
    for copy in in_copies:
        copy.start()
    own_copies = [
        pltpu.make_async_copy(gate, weights.at[core, 0], w_local.at[0]),
        pltpu.make_async_copy(up, weights.at[core, 1], w_local.at[1]),
        pltpu.make_async_copy(down, weights_down.at[:, core], w_local.at[2]),
    ]
    for copy in own_copies:
        copy.start()
    for copy in in_copies:
        copy.wait()
    pack(own_tokens, own_teacher, own_weight, own_routes, own_twin, pay_rows, pay_target)
    pltpu.make_async_copy(pay_rows.at[chip], rows.at[0, 0], rows_recv.at[0]).start()
    pltpu.make_async_copy(pay_target.at[chip], target.at[0], target_recv.at[0]).start()
    pl.semaphore_wait(barrier, chips - 1 + count_y - 1 + 1)

    def send_rows(number):
        def send(step, carry):
            to = peer(step)
            remote(
                pay_rows.at[to], rows.at[0, step], rows_send, rows_recv.at[number], (to * 2 + core, y)
            ).start()
            return carry

        first, count = chunks[number]
        lax.fori_loop(max(first, 1), first + count, send, 0)

    def send_target(part):
        def send(step, carry):
            to = peer(step)
            remote(
                pay_target.at[to], target.at[step], target_send, target_recv.at[part], (to * 2 + core, y)
            ).start()
            return carry

        lax.fori_loop(max(part * part_chips, 1), (part + 1) * part_chips, send, 0)

    for number in range(len(chunks)):
        send_rows(number)
    weight_copies = [
        remote(gate, weights.at[core, 0], w_send.at[0], w_recv.at[0], sibling),
        remote(up, weights.at[core, 1], w_send.at[1], w_recv.at[1], sibling),
        remote(down, weights_down.at[:, core], w_send.at[2], w_recv.at[2], sibling),
    ]
    for copy in weight_copies:
        copy.start()
    send_target(0)
    send_target(1)

    def send_own(number):
        at = pl.ds(*chunks[number])
        await_bytes(rows.at[0, at], rows_recv.at[number])
        remote(rows.at[0, at], rows.at[3, at], ring_send.at[0], left_recv.at[number], right).start()
        remote(rows.at[0, at], rows.at[1, at], ring_send.at[1], right_recv.at[number], left).start()

    def forward(number):
        start, count = chunks[number]
        at, first, last = pl.ds(start, count), pl.ds(start, count // 2), pl.ds(start + count // 2, count // 2)
        await_bytes(rows.at[3, at], left_recv.at[number])
        remote(rows.at[3, first], rows.at[2, first], ring_send.at[2], fwd_left_recv.at[number], right).start()
        await_bytes(rows.at[1, at], right_recv.at[number])
        remote(rows.at[1, last], rows.at[2, last], ring_send.at[3], fwd_right_recv.at[number], left).start()

    def project(part):
        start = part * part_chips
        for number, (first, count) in enumerate(chunks):
            if start <= first < start + part_chips:
                await_bytes(rows.at[2, pl.ds(first, count // 2)], fwd_left_recv.at[number])
                await_bytes(rows.at[2, pl.ds(first + count // 2, count // 2)], fwd_right_recv.at[number])
        pre[...] = jnp.zeros_like(pre)

        def add(rel, carry):
            cls = lax.rem(y + rel, 4)
            block = rows[rel, pl.ds(start, part_chips)].reshape(part_chips * height, feature)
            for half in range(2):
                w = weights[:, :, :, slice_of(cls + 4 * half)].reshape(4 * units, feature)
                pre[half] += lax.dot_general(block, w, NT_DIMS, preferred_element_type=F32)
            return carry

        lax.fori_loop(0, 4, add, 0)
        low = pre[0].reshape(part_chips, height, 4 * units)[:, :group]
        high = pre[1].reshape(part_chips, height, 4 * units)[:, group:]
        slots_pre[:, : 4 * units] = (low + high).reshape(part_slots, 4 * units)
        gates = slots_pre[...].T[: 4 * units].reshape(2, 2, units, part_slots)
        gate_pre = gates[:, 0].reshape(2 * units, part_slots)
        up_pre = gates[:, 1].reshape(2 * units, part_slots)
        sig = 1.0 / (1.0 + jnp.exp(-gate_pre))
        silu = gate_pre * sig
        hidden[part, y] = (silu * up_pre).astype(BF)

        def send_hidden(step, carry):
            to = lax.rem(y + step, count_y)
            remote(hidden.at[part, y], hidden.at[part, y], hid_send, hid_recv.at[part], (me, to)).start()
            return carry

        lax.fori_loop(1, count_y, send_hidden, 0)
        return silu, up_pre * sig * (1.0 + gate_pre * (1.0 - sig))

    def errors(part):
        await_bytes(target.at[pl.ds(part * part_chips, part_chips)], target_recv.at[part])
        await_bytes(hidden.at[part, pl.ds(0, count_y - 1)], hid_recv.at[part])
        all_hidden = hidden[part].reshape(count_y * 2 * units, part_slots)
        all_down = weights_down[...].reshape(count_y * 2 * units, feature)
        out = lax.dot_general(all_hidden, all_down, TN_DIMS, preferred_element_type=F32)
        arrived = target[pl.ds(part * part_chips, part_chips)].astype(F32)
        goal_low = arrived[:, :group].reshape(part_slots, width)
        goal_high = arrived[:, group:].reshape(part_slots, width)
        slot_weight = goal_high[:, tail : tail + 1]
        err[part, :, :width] = (slot_weight * (out[:, :width] - goal_low)).astype(BF)
        err[part, :, width:] = (slot_weight * (out[:, width:] - goal_high[:, :tail])).astype(BF)

        def send_back(step, carry):
            to = lax.rem(y + step, count_y)
            w = weights_down[to].reshape(2 * units, feature)
            back_out[part, to] = lax.dot_general(
                w, err[part], NT_DIMS, preferred_element_type=F32).astype(BF)

            @pl.when(step < count_y)
            def _():
                remote(
                    back_out.at[part, to], back_in.at[part, y], back_send, back_recv.at[part], (me, to)
                ).start()
            return carry

        lax.fori_loop(1, count_y + 1, send_back, 0)

    def back(part, silu, slope):
        await_bytes(back_in.at[part, pl.ds(0, count_y - 1)], back_recv.at[part])

        def add_back(step, total):
            return total + back_in[part, lax.rem(y + step, count_y)].astype(F32)

        back_hidden = lax.fori_loop(1, count_y, add_back, back_out[part, y].astype(F32))
        back_gate = (back_hidden * slope).astype(BF).reshape(2, 1, units, part_slots)
        back_up = (back_hidden * silu).astype(BF).reshape(2, 1, units, part_slots)
        backs = jnp.concatenate([back_gate, back_up], axis=1).reshape(4 * units, part_slots)
        wide = (part_slots, part_chips * height)
        for half in range(2):
            slot_id, lane = iota(wide, 0), iota(wide, 1)
            match = (lane // height == slot_id // group) & (
                lane % height == slot_id % group + group * half)
            expand[half] = jnp.dot(backs, hot(match), preferred_element_type=F32).astype(BF)

    def class_term(rel, part):
        lhs = expand[...].reshape(8 * units, part_chips * height)
        block = rows[rel, pl.ds(part * part_chips, part_chips)].reshape(part_chips * height, feature)
        return jnp.dot(lhs, block, preferred_element_type=F32)

    slots_pre[...] = jnp.zeros_like(slots_pre)
    send_own(0)
    for copy in own_copies + weight_copies:
        copy.wait()
    first_part = len(halves[0])
    for number in range(len(chunks)):
        if number + 1 < len(chunks):
            send_own(number + 1)
        forward(number)
        if number == first_part:
            saved = project(0)
        if number == first_part + 1:
            errors(0)
    if first_part + 1 >= len(chunks):
        errors(0)
    saved_last = project(1)

    back(0, *saved)

    def first_term(rel, carry):
        kept[rel] = class_term(rel, 0)
        return carry

    lax.fori_loop(0, 4, first_term, 0)
    errors(1)

    def down_part(number, carry):
        term = jnp.dot(hidden[0, number], err[0], preferred_element_type=F32) + jnp.dot(
            hidden[1, number], err[1], preferred_element_type=F32)
        down_part_both[...] = term.reshape(2, units, feature)
        down_out[number] = down_part_both[other].astype(BF)
        down_kept[number] = down_part_both[core].astype(BF)
        return carry

    lax.fori_loop(0, count_y, down_part, 0)
    down_copy = remote(down_out, down_in, down_send, down_recv, sibling)
    down_copy.start()

    back(1, *saved_last)

    def class_part(rel, carry):
        cls = lax.rem(y + rel, 4)
        gate_both[...] = (kept[rel] + class_term(rel, 1)).reshape(2, 2, 2 * units, feature)
        gate_out[cls] = gate_both[:, other].astype(BF)
        gate_own[cls] = gate_both[:, core].astype(BF)
        remote(gate_out.at[cls], gate_in.at[cls], gate_send, gate_recv.at[rel], sibling).start()
        return carry

    lax.fori_loop(0, 4, class_part, 0)
    down_copy.wait()
    for rel in range(4):
        await_bytes(gate_in.at[rel], gate_recv.at[rel])

    await_bytes(pay_rows.at[pl.ds(0, chips - 1)], rows_send)
    await_bytes(pay_target.at[pl.ds(0, chips - 1)], target_send)
    await_bytes(rows.at[0], ring_send.at[0])
    await_bytes(rows.at[0], ring_send.at[1])
    await_bytes(rows.at[0, pl.ds(0, chips // 2)], ring_send.at[2])
    await_bytes(rows.at[0, pl.ds(0, chips // 2)], ring_send.at[3])
    for part in range(2):
        await_bytes(hidden.at[part, pl.ds(0, count_y - 1)], hid_send)
        await_bytes(back_out.at[part, pl.ds(0, count_y - 1)], back_send)
    await_bytes(gate_out, gate_send)


def sum_kernel(gate_own, gate_in, down_kept, down_in, grad_gate, grad_up, grad_down):
    units = grad_gate.shape[0]
    feature = gate_own.shape[3]
    for half in range(2):
        for cls in range(4):
            at = pl.ds((cls + 4 * half) * feature, feature)
            total = (gate_own[cls, half].astype(F32) + gate_in[cls, half].astype(F32)).astype(BF)
            grad_gate[:, at] = total[:units]
            grad_up[:, at] = total[units:]
    grad_down[...] = (down_kept[...].astype(F32) + down_in[...].astype(F32)).astype(BF)


def body(
    tokens, teacher_out, route_weight, routes, twin_map, student_gate, student_up, student_down
):
    block, topk = routes.shape
    teachers = twin_map.shape[0]
    chips = teachers // 2
    cap = 2 * block * topk // teachers
    height = 4 * cap
    feature = teacher_out.shape[2]
    width = target_width(feature)
    model = tokens.shape[1]
    units = student_gate.shape[1]
    count_y = model // feature
    slots = chips * 2 * cap
    vmem = pl.BlockSpec(memory_space=pltpu.VMEM)
    anywhere = pl.BlockSpec(memory_space=pl.ANY)
    dma = pltpu.SemaphoreType.DMA
    chunks = sum(len(part) for part in ring_chunks(chips))
    parts = pl.pallas_call(
        main_kernel,
        out_shape=(
            jax.ShapeDtypeStruct((4, 2, 2 * units, feature), BF),
            jax.ShapeDtypeStruct((4, 2, 2 * units, feature), BF),
            jax.ShapeDtypeStruct((count_y, units, feature), BF),
            jax.ShapeDtypeStruct((count_y, units, feature), BF),
        ),
        in_specs=[anywhere] * 8,
        out_specs=(vmem, vmem, vmem, vmem),
        scratch_shapes=[
            pltpu.VMEM((2 * block, feature), BF),
            pltpu.VMEM((block * topk, feature), BF),
            pltpu.VMEM((topk, block), BF),
            pltpu.VMEM((topk, block), jnp.int32),
            pltpu.VMEM((1, teachers), jnp.int32),
            pltpu.VMEM((chips, height, feature), BF),
            pltpu.VMEM((chips, height, width), BF),
            pltpu.VMEM((4, chips, height, feature), BF),
            pltpu.VMEM((chips, height, width), BF),
            pltpu.VMEM((2, 2, units, model), BF),
            pltpu.VMEM((count_y, 2, units, feature), BF),
            pltpu.VMEM((2, chips // 2 * height, 4 * units), F32),
            pltpu.VMEM((slots // 2, -(-4 * units // 128) * 128), F32),
            pltpu.VMEM((2, count_y, 2 * units, slots // 2), BF),
            pltpu.VMEM((2, slots // 2, feature), BF),
            pltpu.VMEM((2, count_y, 2 * units, slots // 2), BF),
            pltpu.VMEM((2, count_y, 2 * units, slots // 2), BF),
            pltpu.VMEM((count_y, units, feature), BF),
            pltpu.VMEM((2, units, feature), F32),
            pltpu.VMEM((2, 4 * units, chips // 2 * height), BF),
            pltpu.VMEM((4, 8 * units, feature), F32),
            pltpu.VMEM((4, 2, 2 * units, feature), BF),
            pltpu.VMEM((2, 2, 2 * units, feature), F32),
            dma((6,)), dma((3,)), dma((3,)), dma((3,)),
            dma((chunks,)), dma, dma((2,)), dma,
            dma((chunks,)), dma((chunks,)), dma((chunks,)), dma((chunks,)), dma((4,)),
            dma, dma((2,)), dma, dma((2,)), dma, dma, dma, dma((4,)),
        ],
        compiler_params=pltpu.CompilerParams(
            collective_id=0, has_side_effects=True, vmem_limit_bytes=60 * 1024 * 1024),
    )(
        tokens, teacher_out.reshape(block * topk, feature), route_weight.T, routes.T,
        twin_map.reshape(1, teachers), student_gate[0], student_up[0],
        student_down[0].reshape(count_y, units, feature),
    )
    grads = pl.pallas_call(
        sum_kernel,
        out_shape=(
            jax.ShapeDtypeStruct((units, model), BF),
            jax.ShapeDtypeStruct((units, model), BF),
            jax.ShapeDtypeStruct((count_y, units, feature), BF),
        ),
        in_specs=[vmem] * 4,
        out_specs=(vmem, vmem, vmem),
        compiler_params=pltpu.CompilerParams(vmem_limit_bytes=60 * 1024 * 1024),
    )(*parts)
    return (
        grads[0][None], grads[1][None], grads[2].reshape(1, count_y * units, feature))


def solution(mesh):
    placed = (
        P("expert", None),
        P("expert", None, "dp"),
        P("expert", None),
        P("expert", None),
        P(),
        P("expert", "dp", None),
        P("expert", "dp", None),
        P("expert", None, "dp"),
    )
    return jax.shard_map(
        body,
        mesh=mesh,
        in_specs=placed,
        out_specs=(P("expert", "dp", None), P("expert", "dp", None), P("expert", None, "dp")),
        check_vma=False,
    )
```

time: 96.5 us -> 86.7 us (0.90)
  local copies, waits for them, and re-layouts: 9.35 us -> 0 us
    unnamed x23 -> x0, local copies, waits for them, and re-layouts: 9.26 us -> none
where the time goes in v2:
time: 86.7 us; the launch traced here: 85.6 us
  Pallas kernels  85 us (98%)
    pallas_call x1, Pallas kernels, body(): pl.pallas_call(main_kernel, out_shape=(jax.ShapeDtypeStruct((4, 2, 2 * un...  81.4 us
    pallas_call x1, Pallas kernels, body(): pl.pallas_call(sum_kernel, out_shape=(jax.ShapeDtypeStruct((units, model)...  3.6 us

profile of v2, /device:TPU:1, one launch (start us, length us, event | category | flops | bytes accessed | tf_op | source)
XLA Modules:
  0.0 85.6 jit_solution(4051576854430037434)
XLA Ops:
  0.6 81.4 %shard_map.103 = (bf16[4,2,96,896]{3,2,1,0:T(8,128)(2,1)}, bf16[4,2,96,896]{3,2,1,0:T(8,128)(2,1)}, bf16[8,48,896]{2,1,0:T(8,128)(2,1)}, bf16[8,48,896]{2,1,0:T(8,128)(2,1)}) custom-call(bf16[16,7168]{1,0:T(8,128)(2,1)} %tokens.1, bf16[128,896]{1,0:T(8,128)(2,1)} %bitcast.13, bf16[8,16]{1,0:T(8,128)(2,1)} %bitcast.15, s32[8,16]{1,0:T(8,128)} %bitcast.14, ...), custom_call_target="tpu_custom_call" | custom-call | tf_op jit(solution)/shard_map/pallas_call | solution.py:423
  82.0 3.6 %shard_map.104 = (bf16[48,7168]{1,0:T(8,128)(2,1)}, bf16[48,7168]{1,0:T(8,128)(2,1)}, bf16[8,48,896]{2,1,0:T(8,128)(2,1)}) custom-call(bf16[4,2,96,896]{3,2,1,0:T(8,128)(2,1)} %get-tuple-element.10.gate_own, bf16[4,2,96,896]{3,2,1,0:T(8,128)(2,1)} %get-tuple-element.11.gate_in, bf16[8,48,896]{2,1,0:T(8,128)(2,1)} %get-tuple-element.12.down_kept, ...), custom_call_target="tpu_custom_call" | custom-call | tf_op jit(solution)/shard_map/pallas_call | solution.py:469

commit v3 on v2

--- a/solution.py
+++ b/solution.py
@@ -37,7 +37,7 @@
     return halves
 
 
-def pack(tokens, teacher, weight, routes, twin, pay_rows, pay_target):
+def pack(tokens, teacher, weight, routes, twin, pay_rows, pay_more, pay_target):
     topk, block = routes.shape
     pairs = block * topk
     teachers = twin.shape[1]
@@ -85,8 +85,10 @@
     pick = jnp.dot(hot(filled), spread, preferred_element_type=F32)
     pick_half = iota((rows, 2 * block), 1) // block == (iota((rows, 2 * block), 0) // group) % 2
     pick = jnp.where(pick_half, pick, 0.0).astype(BF)
-    sent = jnp.dot(pick, tokens[...], preferred_element_type=F32).astype(BF)
-    pay_rows[...] = sent.reshape(pay_rows.shape)
+    for number, pay in enumerate((pay_rows, pay_more)):
+        both = tokens[pl.ds(number * 2 * block, 2 * block), :]
+        sent = jnp.dot(pick, both, preferred_element_type=F32).astype(BF)
+        pay[...] = sent.reshape(pay.shape)
 
     spread_weight = jnp.broadcast_to(weight_col, (pairs, 128)).astype(BF)
     tail = jnp.concatenate([teacher[:, width:], spread_weight], axis=1)
@@ -98,10 +100,11 @@
 def main_kernel(
     tokens, teacher, weight, routes, twin, gate, up, down,
     gate_own, gate_in, down_kept, down_in,
-    own_tokens, own_teacher, own_weight, own_routes, own_twin, pay_rows, pay_target, rows, target, weights, weights_down, pre, slots_pre, hidden, err, back_out, back_in,
-    down_out, down_part_both, expand, kept, gate_out, gate_both,
+    own_tokens, own_teacher, own_weight, own_routes, own_twin, pay_rows, pay_more, pay_target, rows, target, weights, weights_down, pre, slots_pre, hidden, err, back_out, back_in,
+    down_out, down_mine, down_part_both, expand, kept, gate_out, gate_mine, gate_both,
     in_local, w_recv, w_local, w_send, rows_recv, rows_send, target_recv, target_send,
     left_recv, right_recv, fwd_left_recv, fwd_right_recv, ring_send,
+    more_send, more_recv, out_sem,
     hid_send, hid_recv, back_send, back_recv, down_send, down_recv, gate_send, gate_recv,
 ):
     chips = pay_rows.shape[0]
@@ -129,6 +132,8 @@
     left = (me, left_y)
 
     def peer(step):
+        if isinstance(step, int):
+            return to_x[step % XS] + to_z[step // XS]
         dx = lax.rem(step, XS)
         turn = step // XS
         dz = jnp.where(lax.rem(turn, 2) == 1, (turn + 1) // 2, line - turn // 2)
@@ -136,6 +141,7 @@
 
     halves = ring_chunks(chips)
     chunks = halves[0] + halves[1]
+    direct = sum(halves[0][min(1, len(halves[0]) - 1)])
     part_chips = chips // 2
     part_slots = slots // 2
 
@@ -168,14 +174,17 @@
             device_id_type=pl.DeviceIdType.MESH)
 
     cls = lax.rem(y, 4)
+    far = lax.rem(y + 2, 4)
     in_copies = [
-        pltpu.make_async_copy(tokens.at[:, slice_of(cls)], own_tokens.at[pl.ds(0, block)], in_local.at[0]),
         pltpu.make_async_copy(
-            tokens.at[:, slice_of(cls + 4)], own_tokens.at[pl.ds(block, block)], in_local.at[1]),
-        pltpu.make_async_copy(teacher, own_teacher, in_local.at[2]),
-        pltpu.make_async_copy(weight, own_weight, in_local.at[3]),
-        pltpu.make_async_copy(routes, own_routes, in_local.at[4]),
-        pltpu.make_async_copy(twin, own_twin, in_local.at[5]),
+            tokens.at[:, slice_of(first)], own_tokens.at[pl.ds(number * block, block)],
+            in_local.at[4 + number])
+        for number, first in enumerate((cls, cls + 4, far, far + 4))
+    ] + [
+        pltpu.make_async_copy(teacher, own_teacher, in_local.at[0]),
+        pltpu.make_async_copy(weight, own_weight, in_local.at[1]),
+        pltpu.make_async_copy(routes, own_routes, in_local.at[2]),
+        pltpu.make_async_copy(twin, own_twin, in_local.at[3]),
     ]
     for copy in in_copies:
         copy.start()
@@ -188,21 +197,19 @@
         copy.start()
     for copy in in_copies:
         copy.wait()
-    pack(own_tokens, own_teacher, own_weight, own_routes, own_twin, pay_rows, pay_target)
+    pack(own_tokens, own_teacher, own_weight, own_routes, own_twin, pay_rows, pay_more, pay_target)
     pltpu.make_async_copy(pay_rows.at[chip], rows.at[0, 0], rows_recv.at[0]).start()
+    pltpu.make_async_copy(pay_more.at[chip], rows.at[2, 0], more_recv).start()
     pltpu.make_async_copy(pay_target.at[chip], target.at[0], target_recv.at[0]).start()
     pl.semaphore_wait(barrier, chips - 1 + count_y - 1 + 1)
 
     def send_rows(number):
-        def send(step, carry):
+        first, count = chunks[number]
+        for step in range(max(first, 1), first + count):
             to = peer(step)
             remote(
                 pay_rows.at[to], rows.at[0, step], rows_send, rows_recv.at[number], (to * 2 + core, y)
             ).start()
-            return carry
-
-        first, count = chunks[number]
-        lax.fori_loop(max(first, 1), first + count, send, 0)
 
     def send_target(part):
         def send(step, carry):
@@ -214,17 +221,26 @@
 
         lax.fori_loop(max(part * part_chips, 1), (part + 1) * part_chips, send, 0)
 
-    for number in range(len(chunks)):
-        send_rows(number)
+    def send_more():
+        for step in range(1, direct):
+            to = peer(step)
+            remote(
+                pay_more.at[to], rows.at[2, step], more_send, more_recv, (to * 2 + core, y)
+            ).start()
+
     weight_copies = [
         remote(gate, weights.at[core, 0], w_send.at[0], w_recv.at[0], sibling),
         remote(up, weights.at[core, 1], w_send.at[1], w_recv.at[1], sibling),
         remote(down, weights_down.at[:, core], w_send.at[2], w_recv.at[2], sibling),
     ]
-    for copy in weight_copies:
-        copy.start()
-    send_target(0)
-    send_target(1)
+
+    def send_weights():
+        for copy in weight_copies:
+            copy.start()
+
+    def await_weights():
+        for copy in own_copies + weight_copies:
+            copy.wait()
 
     def send_own(number):
         at = pl.ds(*chunks[number])
@@ -234,6 +250,8 @@
 
     def forward(number):
         start, count = chunks[number]
+        if start < direct:
+            return
         at, first, last = pl.ds(start, count), pl.ds(start, count // 2), pl.ds(start + count // 2, count // 2)
         await_bytes(rows.at[3, at], left_recv.at[number])
         remote(rows.at[3, first], rows.at[2, first], ring_send.at[2], fwd_left_recv.at[number], right).start()
@@ -243,20 +261,31 @@
     def project(part):
         start = part * part_chips
         for number, (first, count) in enumerate(chunks):
-            if start <= first < start + part_chips:
-                await_bytes(rows.at[2, pl.ds(first, count // 2)], fwd_left_recv.at[number])
-                await_bytes(rows.at[2, pl.ds(first + count // 2, count // 2)], fwd_right_recv.at[number])
+            if start <= first < min(start + part_chips, direct):
+                await_bytes(rows.at[3, pl.ds(first, count)], left_recv.at[number])
+                await_bytes(rows.at[1, pl.ds(first, count)], right_recv.at[number])
         pre[...] = jnp.zeros_like(pre)
 
-        def add(rel, carry):
+        def add(turn, carry):
+            rel = turn + turn // 2
+            add_class(rel)
+            return carry
+
+        def add_class(rel):
             cls = lax.rem(y + rel, 4)
             block = rows[rel, pl.ds(start, part_chips)].reshape(part_chips * height, feature)
             for half in range(2):
                 w = weights[:, :, :, slice_of(cls + 4 * half)].reshape(4 * units, feature)
                 pre[half] += lax.dot_general(block, w, NT_DIMS, preferred_element_type=F32)
-            return carry
-
-        lax.fori_loop(0, 4, add, 0)
+
+        lax.fori_loop(0, 3, add, 0)
+        if part == 0:
+            await_bytes(rows.at[2, pl.ds(0, direct)], more_recv)
+        for number, (first, count) in enumerate(chunks):
+            if max(start, direct) <= first < start + part_chips:
+                await_bytes(rows.at[2, pl.ds(first, count // 2)], fwd_left_recv.at[number])
+                await_bytes(rows.at[2, pl.ds(first + count // 2, count // 2)], fwd_right_recv.at[number])
+        add_class(2)
         low = pre[0].reshape(part_chips, height, 4 * units)[:, :group]
         high = pre[1].reshape(part_chips, height, 4 * units)[:, group:]
         slots_pre[:, : 4 * units] = (low + high).reshape(part_slots, 4 * units)
@@ -326,20 +355,32 @@
         return jnp.dot(lhs, block, preferred_element_type=F32)
 
     slots_pre[...] = jnp.zeros_like(slots_pre)
+    last = len(chunks) - 1
+    for number in range(last):
+        send_rows(number)
+    send_more()
+    send_rows(last)
     send_own(0)
-    for copy in own_copies + weight_copies:
-        copy.wait()
-    first_part = len(halves[0])
-    for number in range(len(chunks)):
-        if number + 1 < len(chunks):
-            send_own(number + 1)
+    send_weights()
+    for number in range(1, min(3, last + 1)):
+        send_own(number)
+    send_target(0)
+    await_weights()
+    for number in range(min(3, last + 1)):
+        if number == 2:
+            send_own(3)
         forward(number)
-        if number == first_part:
+    send_target(1)
+    for number in range(3, last):
+        send_own(number + 1)
+        forward(number)
+        if number == 3:
             saved = project(0)
-        if number == first_part + 1:
-            errors(0)
-    if first_part + 1 >= len(chunks):
-        errors(0)
+    if last < 4:
+        saved = project(0)
+    if last > 2:
+        forward(last)
+    errors(0)
     saved_last = project(1)
 
     back(0, *saved)
@@ -356,12 +397,14 @@
             hidden[1, number], err[1], preferred_element_type=F32)
         down_part_both[...] = term.reshape(2, units, feature)
         down_out[number] = down_part_both[other].astype(BF)
-        down_kept[number] = down_part_both[core].astype(BF)
+        down_mine[number] = down_part_both[core].astype(BF)
         return carry
 
     lax.fori_loop(0, count_y, down_part, 0)
     down_copy = remote(down_out, down_in, down_send, down_recv, sibling)
     down_copy.start()
+    kept_copy = pltpu.make_async_copy(down_mine, down_kept, out_sem.at[4])
+    kept_copy.start()
 
     back(1, *saved_last)
 
@@ -369,21 +412,26 @@
         cls = lax.rem(y + rel, 4)
         gate_both[...] = (kept[rel] + class_term(rel, 1)).reshape(2, 2, 2 * units, feature)
         gate_out[cls] = gate_both[:, other].astype(BF)
-        gate_own[cls] = gate_both[:, core].astype(BF)
+        gate_mine[rel] = gate_both[:, core].astype(BF)
+        pltpu.make_async_copy(gate_mine.at[rel], gate_own.at[cls], out_sem.at[rel]).start()
         remote(gate_out.at[cls], gate_in.at[cls], gate_send, gate_recv.at[rel], sibling).start()
         return carry
 
     lax.fori_loop(0, 4, class_part, 0)
     down_copy.wait()
+    kept_copy.wait()
     for rel in range(4):
-        await_bytes(gate_in.at[rel], gate_recv.at[rel])
+        cls = lax.rem(y + rel, 4)
+        pltpu.make_async_copy(gate_mine.at[rel], gate_own.at[cls], out_sem.at[rel]).wait()
+        await_bytes(gate_in.at[cls], gate_recv.at[rel])
 
     await_bytes(pay_rows.at[pl.ds(0, chips - 1)], rows_send)
     await_bytes(pay_target.at[pl.ds(0, chips - 1)], target_send)
     await_bytes(rows.at[0], ring_send.at[0])
     await_bytes(rows.at[0], ring_send.at[1])
-    await_bytes(rows.at[0, pl.ds(0, chips // 2)], ring_send.at[2])
-    await_bytes(rows.at[0, pl.ds(0, chips // 2)], ring_send.at[3])
+    await_bytes(rows.at[0, pl.ds(0, (chips - direct) // 2)], ring_send.at[2])
+    await_bytes(rows.at[0, pl.ds(0, (chips - direct) // 2)], ring_send.at[3])
+    await_bytes(pay_more.at[pl.ds(0, direct - 1)], more_send)
     for part in range(2):
         await_bytes(hidden.at[part, pl.ds(0, count_y - 1)], hid_send)
         await_bytes(back_out.at[part, pl.ds(0, count_y - 1)], back_send)
@@ -429,13 +477,14 @@
             jax.ShapeDtypeStruct((count_y, units, feature), BF),
         ),
         in_specs=[anywhere] * 8,
-        out_specs=(vmem, vmem, vmem, vmem),
+        out_specs=(anywhere,) * 4,
         scratch_shapes=[
-            pltpu.VMEM((2 * block, feature), BF),
+            pltpu.VMEM((4 * block, feature), BF),
             pltpu.VMEM((block * topk, feature), BF),
             pltpu.VMEM((topk, block), BF),
             pltpu.VMEM((topk, block), jnp.int32),
             pltpu.VMEM((1, teachers), jnp.int32),
+            pltpu.VMEM((chips, height, feature), BF),
             pltpu.VMEM((chips, height, feature), BF),
             pltpu.VMEM((chips, height, width), BF),
             pltpu.VMEM((4, chips, height, feature), BF),
@@ -449,14 +498,17 @@
             pltpu.VMEM((2, count_y, 2 * units, slots // 2), BF),
             pltpu.VMEM((2, count_y, 2 * units, slots // 2), BF),
             pltpu.VMEM((count_y, units, feature), BF),
+            pltpu.VMEM((count_y, units, feature), BF),
             pltpu.VMEM((2, units, feature), F32),
             pltpu.VMEM((2, 4 * units, chips // 2 * height), BF),
             pltpu.VMEM((4, 8 * units, feature), F32),
             pltpu.VMEM((4, 2, 2 * units, feature), BF),
+            pltpu.VMEM((4, 2, 2 * units, feature), BF),
             pltpu.VMEM((2, 2, 2 * units, feature), F32),
-            dma((6,)), dma((3,)), dma((3,)), dma((3,)),
+            dma((8,)), dma((3,)), dma((3,)), dma((3,)),
             dma((chunks,)), dma, dma((2,)), dma,
             dma((chunks,)), dma((chunks,)), dma((chunks,)), dma((chunks,)), dma((4,)),
+            dma, dma, dma((5,)),
             dma, dma((2,)), dma, dma((2,)), dma, dma, dma, dma((4,)),
         ],
         compiler_params=pltpu.CompilerParams(

time: 86.7 us -> 79.9 us (0.922); the launches traced: 85.6 us -> 79.7 us
  Pallas kernels: 85 us -> 79.1 us
    pallas_call x1, Pallas kernels: 81.4 us -> 75.5 us  [body(): pl.pallas_call(main_kernel, out_shape=(jax.ShapeDtypeStruct((4, 2, 2 * un...]
where the time goes in v3:
time: 79.9 us; the launch traced here: 79.7 us
  Pallas kernels  79.1 us (99%)
    pallas_call x1, Pallas kernels, body(): pl.pallas_call(main_kernel, out_shape=(jax.ShapeDtypeStruct((4, 2, 2 * un...  75.5 us
    pallas_call x1, Pallas kernels, body(): pl.pallas_call(sum_kernel, out_shape=(jax.ShapeDtypeStruct((units, model)...  3.6 us

profile of v3, /device:TPU:1, one launch (start us, length us, event | category | flops | bytes accessed | tf_op | source)
XLA Modules:
  0.0 79.7 jit_solution(8653374488548713664)
XLA Ops:
  0.6 75.5 %shard_map.103 = (bf16[4,2,96,896]{3,2,1,0:T(8,128)(2,1)}, bf16[4,2,96,896]{3,2,1,0:T(8,128)(2,1)}, bf16[8,48,896]{2,1,0:T(8,128)(2,1)}, bf16[8,48,896]{2,1,0:T(8,128)(2,1)}) custom-call(bf16[16,7168]{1,0:T(8,128)(2,1)} %tokens.1, bf16[128,896]{1,0:T(8,128)(2,1)} %bitcast.13, bf16[8,16]{1,0:T(8,128)(2,1)} %bitcast.15, s32[8,16]{1,0:T(8,128)} %bitcast.14, ...), custom_call_target="tpu_custom_call" | custom-call | tf_op jit(solution)/shard_map/pallas_call | solution.py:471
  76.1 3.6 %shard_map.104 = (bf16[48,7168]{1,0:T(8,128)(2,1)}, bf16[48,7168]{1,0:T(8,128)(2,1)}, bf16[8,48,896]{2,1,0:T(8,128)(2,1)}) custom-call(bf16[4,2,96,896]{3,2,1,0:T(8,128)(2,1)} %get-tuple-element.10.gate_own, bf16[4,2,96,896]{3,2,1,0:T(8,128)(2,1)} %get-tuple-element.11.gate_in, bf16[8,48,896]{2,1,0:T(8,128)(2,1)} %get-tuple-element.12.down_kept, ...), custom_call_target="tpu_custom_call" | custom-call | tf_op jit(solution)/shard_map/pallas_call | solution.py:521

commit v4 on v3

--- a/solution.py
+++ b/solution.py
@@ -370,13 +370,14 @@
         if number == 2:
             send_own(3)
         forward(number)
-    send_target(1)
     for number in range(3, last):
         send_own(number + 1)
         forward(number)
         if number == 3:
+            send_target(1)
             saved = project(0)
     if last < 4:
+        send_target(1)
         saved = project(0)
     if last > 2:
         forward(last)

time: 79.9 us -> 80.1 us (level)
  no operation moved by 1% of the time
where the time goes in v4:
time: 80.1 us; the launch traced here: 79.9 us
  Pallas kernels  79.3 us (99%)
    pallas_call x1, Pallas kernels, body(): pl.pallas_call(main_kernel, out_shape=(jax.ShapeDtypeStruct((4, 2, 2 * un...  75.7 us
    pallas_call x1, Pallas kernels, body(): pl.pallas_call(sum_kernel, out_shape=(jax.ShapeDtypeStruct((units, model)...  3.6 us

profile of v4, /device:TPU:1, one launch (start us, length us, event | category | flops | bytes accessed | tf_op | source)
XLA Modules:
  0.0 79.9 jit_solution(16506436907079244639)
XLA Ops:
  0.6 75.7 %shard_map.103 = (bf16[4,2,96,896]{3,2,1,0:T(8,128)(2,1)}, bf16[4,2,96,896]{3,2,1,0:T(8,128)(2,1)}, bf16[8,48,896]{2,1,0:T(8,128)(2,1)}, bf16[8,48,896]{2,1,0:T(8,128)(2,1)}) custom-call(bf16[16,7168]{1,0:T(8,128)(2,1)} %tokens.1, bf16[128,896]{1,0:T(8,128)(2,1)} %bitcast.13, bf16[8,16]{1,0:T(8,128)(2,1)} %bitcast.15, s32[8,16]{1,0:T(8,128)} %bitcast.14, ...), custom_call_target="tpu_custom_call" | custom-call | tf_op jit(solution)/shard_map/pallas_call | solution.py:472
  76.3 3.6 %shard_map.104 = (bf16[48,7168]{1,0:T(8,128)(2,1)}, bf16[48,7168]{1,0:T(8,128)(2,1)}, bf16[8,48,896]{2,1,0:T(8,128)(2,1)}) custom-call(bf16[4,2,96,896]{3,2,1,0:T(8,128)(2,1)} %get-tuple-element.10.gate_own, bf16[4,2,96,896]{3,2,1,0:T(8,128)(2,1)} %get-tuple-element.11.gate_in, bf16[8,48,896]{2,1,0:T(8,128)(2,1)} %get-tuple-element.12.down_kept, ...), custom_call_target="tpu_custom_call" | custom-call | tf_op jit(solution)/shard_map/pallas_call | solution.py:522
